TPU v7x, 32 devices: a whole 2x2x4 slice. The times are simulated.
32 devices in a mesh: runs: 2 (over x), area: 16 (over z, y, core).
Axes of the slice: x: 2, y: 2, z: 4, core: 2. Of those that a mesh axis runs over, the one named last changes fastest.
Arguments:
- history: bfloat16 [4, 32, 16384], P(None, 'runs', 'area'), parts along dimension 1, may hold values from 0 to 1
- drive: bfloat16 [32, 16384], P('runs', 'area'), parts along dimension 0, may hold values from -6 to 6
- leak: float32 [32768], P(('runs', 'area')), parts along dimension 0, may hold values from 0.1 to 0.9
- inhibition: float32 [16], P('runs'), parts along dimension 0, may hold values from 0.5 to 4
- section: int32 [16], replicated, may hold values from 0 to 7, never falling along the last dimension, each value on 1 to 6 neighbouring positions
- link_source: int32 [768, 1], P('area'), may hold values from 0 to 15; in each aligned block of 48 rows (0 to 47, 48 to 95, ...) at most 3 rows name the same one
- link_block: int32 [768], P('area'), may hold values from 0 to 3
- link_target: int32 [768], P('area'), may hold values from 0 to 3
- link_delay: int32 [768], P('area'), may hold values from 2 to 4
- remote_weight: bfloat16 [1536, 256, 256], P(('runs', 'area')), parts along dimension 0, may hold values from -0.375 to 0.375
- local_block: int32 [256], P('area'), may hold values from 0 to 3
- local_target: int32 [256], P('area'), may hold values from 0 to 3
- local_delay: int32 [256], P('area'), may hold values from 1 to 4
- local_weight: bfloat16 [512, 256, 256], P(('runs', 'area')), parts along dimension 0, may hold values from -0.375 to 0.375
Outputs:
- rates: bfloat16 [32, 16384], P('runs', 'area'), parts along dimension 0
There are 2 independent parts, one for each index of `runs`. A program takes and returns all parts, laid end to end along the dimension named above; an argument that names none is the same for every part. Nothing has to cross between parts.
Inputs may be any that keep to these rules, and one draw needn't show every extreme that they name: `section`: Nondecreasing; every area covers 1 to 6 consecutive indices, and some area covers exactly 6. `link_source`: among the 48 remote tiles of one index of area, no index of area is named more than 3 times, a bound that some block reaches.
All inputs are finite; a program needn't handle non-finite values.
Results may differ from a plain program's by a relative error of at most 0.005.
Values may be sent and summed in bfloat16 or wider, within the bound.
A program may use at most 128 MiB of HBM per device.

v0:
```python
import jax
import jax.numpy as jnp
from jax import lax
from jax.sharding import PartitionSpec as P

STEPS = 6


def local(
    history,
    drive,
    leak,
    inhibition,
    section,
    link_source,
    link_block,
    link_target,
    link_delay,
    remote_weight,
    local_block,
    local_target,
    local_delay,
    local_weight,
):
    delay_depth, trials, row_width = history.shape
    pop_size = remote_weight.shape[1]
    blocks = row_width // pop_size
    link_count = link_block.shape[0]
    devices = lax.axis_size("area")
    capacity = max(2, (link_count + devices - 1) // devices)
    slot_total = devices * capacity
    area_total = inhibition.shape[0]
    state_rows = (
        history.reshape(delay_depth, trials, blocks, pop_size)
        .transpose(0, 2, 1, 3)
        .reshape(delay_depth * blocks, trials, pop_size)
    )
    source = link_source[:, 0]
    positions = jnp.arange(link_count, dtype=jnp.int32)
    earlier = (source[:, None] == source[None, :]) & (positions[None, :] < positions[:, None])
    slot_rank = jnp.sum(earlier.astype(jnp.int32), axis=1)
    slot_index = source * capacity + slot_rank
    slot_table = slot_index[:, None] == jnp.arange(slot_total, dtype=jnp.int32)[None, :]
    slot_used = jnp.any(slot_table, axis=0)
    want_block = jnp.sum(jnp.where(slot_table, link_block[:, None], 0), axis=0)
    want_delay = jnp.where(
        slot_used, jnp.sum(jnp.where(slot_table, link_delay[:, None], 0), axis=0), delay_depth
    )
    asked_block, asked_delay = (
        lax.all_to_all(
            want_block.reshape(devices, capacity), "area", split_axis=0, concat_axis=0, tiled=True
        ),
        lax.all_to_all(
            want_delay.reshape(devices, capacity), "area", split_axis=0, concat_axis=0, tiled=True
        ),
    )
    asked_block = asked_block.reshape(slot_total)
    asked_delay = asked_delay.reshape(slot_total)
    target_onehot = (link_target[None, :] == jnp.arange(blocks, dtype=jnp.int32)[:, None]).astype(
        jnp.float32
    )
    local_onehot = (local_target[None, :] == jnp.arange(blocks, dtype=jnp.int32)[:, None]).astype(
        jnp.float32
    )
    local_index = (local_delay - 1) * blocks + local_block
    leak_rows = leak.reshape(blocks, pop_size)[:, None, :]
    drive_blocks = drive.astype(jnp.float32).reshape(trials, blocks, pop_size).transpose(1, 0, 2)
    my_index = lax.axis_index("area")
    my_area = lax.dynamic_slice_in_dim(section, my_index, 1, 0)[0]
    area_mask = jnp.arange(area_total, dtype=jnp.int32) == my_area
    area_count = jnp.sum((section == my_area).astype(jnp.float32)) * row_width
    inhibit = jnp.sum(jnp.where(area_mask, inhibition, 0.0))
    fresh = state_rows[:blocks]
    for step_index in range(STEPS):
        outgoing = jnp.take(state_rows, (asked_delay - 1) * blocks + asked_block, axis=0).reshape(
            devices, capacity, trials, pop_size
        )
        received = lax.all_to_all(
            outgoing, "area", split_axis=0, concat_axis=0, tiled=True
        ).reshape(slot_total, trials, pop_size)
        remote_in = jnp.take(received, slot_index, axis=0)
        previous = state_rows[:blocks].astype(jnp.float32)
        own_sum = jnp.sum(previous, axis=(0, 2))
        area_table = jnp.where(area_mask[:, None], own_sum[None, :], 0.0)
        summed = lax.psum(area_table, "area")
        total_mine = jnp.sum(jnp.where(area_mask[:, None], summed, 0.0), axis=0)
        mean_now = total_mine / area_count
        local_in = jnp.take(state_rows, local_index, axis=0)
        local_terms = jnp.einsum(
            "ltp,lpq->ltq", local_in, local_weight, preferred_element_type=jnp.float32
        )
        remote_terms = jnp.einsum(
            "ltp,lpq->ltq", remote_in, remote_weight, preferred_element_type=jnp.float32
        )
        current = jnp.einsum(
            "bl,ltq->btq", target_onehot, remote_terms, precision=lax.Precision.HIGHEST
        )
        current = current + jnp.einsum(
            "bl,ltq->btq", local_onehot, local_terms, precision=lax.Precision.HIGHEST
        )
        driven = jax.nn.sigmoid(current + drive_blocks - inhibit * mean_now[None, :, None])
        fresh = ((1.0 - leak_rows) * previous + leak_rows * driven).astype(jnp.bfloat16)
        state_rows = jnp.concatenate([fresh, state_rows[:-blocks]], axis=0)
    return fresh.transpose(1, 0, 2).reshape(trials, row_width)


def solution(mesh):
    placed = (
        P(None, "runs", "area"),
        P("runs", "area"),
        P(("runs", "area")),
        P("runs"),
        P(),
        P("area", None),
        P("area"),
        P("area"),
        P("area"),
        P(("runs", "area"), None, None),
        P("area"),
        P("area"),
        P("area"),
        P(("runs", "area"), None, None),
    )
    return jax.shard_map(
        local, mesh=mesh, in_specs=placed, out_specs=P("runs", "area"), check_vma=False
    )
```

profile of v0, /device:TPU:0, one launch (start us, length us, event | category | flops | bytes accessed | tf_op | source)
XLA Modules:
  0.0 361.1 jit_solution(18329687779567038272)
XLA Ops:
  3.1 7.4 %all-to-all-start.1 = ((s32[16,1,3]{2,1,0:T(1,128)}), s32[16,1,3]{2,1,0:T(1,128)S(1)}, u32[]{:S(2)}, u32[]{:S(2)}) async-start(s32[16,1,3]{2,1,0:T(1,128)} %bitcast.6), calls=%async_computation.1 | async-start | bytes 16384 | tf_op jit(solution)/shard_map/all_to_all | solution.py:50
  17.9 33.8 %psum.42 = f32[8,16]{1,0:T(8,128)S(1)} all-reduce(f32[8,16]{1,0:T(8,128)S(1)} %broadcast_select_fusion.11), channel_id=1, replica_groups=mesh['runs'=2,'area'=16] {'area'}, use_global_device_ids=true, to_apply=%region_7.11 | all-reduce | flops 128 | bytes 1024 | tf_op jit(solution)/shard_map/psum | solution.py:85
  59.9 4.4 %all-to-all-done = s32[16,1,3]{2,1,0:T(1,128)S(1)} async-done(((s32[16,1,3]{2,1,0:T(1,128)}), s32[16,1,3]{2,1,0:T(1,128)S(1)}, u32[]{:S(2)}, u32[]{:S(2)}) %all-to-all-start) | async-done | bytes 224 | tf_op jit(solution)/shard_map/all_to_all | solution.py:53
  65.9 3.6 all-to-all-start.2
  71.6 10.1 %all-to-all-done.2 = bf16[16,3,16,256]{3,2,1,0:T(8,128)(2,1)S(1)} async-done(((bf16[16,3,16,256]{3,2,1,0:T(8,128)(2,1)}), bf16[16,3,16,256]{3,2,1,0:T(8,128)(2,1)S(1)}, u32[]{:S(2)}, u32[]{:S(2)}) %all-to-all-start.2) | async-done | bytes 393248 | tf_op jit(solution)/shard_map/all_to_all | solution.py:78
  82.2 3.8 %fusion.70 = f32[48,16,256]{2,1,0:T(8,128)S(1)} fusion(bf16[48,256,256]{2,1,0:T(8,128)(2,1)} %param.29, bf16[48,16,256]{2,1,0:T(8,128)(2,1)S(1)} %gather_fusion.1, pred[48]{0:T(512)(128)(4,1)S(1)} %get-tuple-element.10), kind=kOutput, calls=%fused_computation.94 | convolution fusion | flops 100859904 | bytes 7471152 | tf_op jit(solution)/shard_map/ltp,lpq->ltq/dot_general | solution.py:92
  88.3 31.4 %psum.43 = f32[8,16]{1,0:T(8,128)S(1)} all-reduce(f32[8,16]{1,0:T(8,128)S(1)} %broadcast_select_fusion.10), channel_id=1, replica_groups=mesh['runs'=2,'area'=16] {'area'}, use_global_device_ids=true, to_apply=%region_11.15 | all-reduce | flops 128 | bytes 1024 | tf_op jit(solution)/shard_map/psum | solution.py:85
  120.7 3.6 all-to-all-start.3
  125.7 10.7 %all-to-all-done.3 = bf16[16,3,16,256]{3,2,1,0:T(8,128)(2,1)S(1)} async-done(((bf16[16,3,16,256]{3,2,1,0:T(8,128)(2,1)}), bf16[16,3,16,256]{3,2,1,0:T(8,128)(2,1)S(1)}, u32[]{:S(2)}, u32[]{:S(2)}) %all-to-all-start.3) | async-done | bytes 393248 | tf_op jit(solution)/shard_map/all_to_all | solution.py:78
  137.0 3.7 %fusion.68 = f32[48,16,256]{2,1,0:T(8,128)S(1)} fusion(bf16[48,256,256]{2,1,0:T(8,128)(2,1)} %param.29, bf16[48,16,256]{2,1,0:T(8,128)(2,1)S(1)} %gather_fusion.4, pred[48]{0:T(512)(128)(4,1)S(1)} %get-tuple-element.10), kind=kOutput, calls=%fused_computation.92 | convolution fusion | flops 100859904 | bytes 7471152 | tf_op jit(solution)/shard_map/ltp,lpq->ltq/dot_general | solution.py:92
  143.0 31.4 %psum.44 = f32[8,16]{1,0:T(8,128)S(1)} all-reduce(f32[8,16]{1,0:T(8,128)S(1)} %broadcast_select_fusion.9), channel_id=1, replica_groups=mesh['runs'=2,'area'=16] {'area'}, use_global_device_ids=true, to_apply=%region_14.18 | all-reduce | flops 128 | bytes 1024 | tf_op jit(solution)/shard_map/psum | solution.py:85
  175.4 3.6 all-to-all-start.4
  180.4 10.7 %all-to-all-done.4 = bf16[16,3,16,256]{3,2,1,0:T(8,128)(2,1)S(1)} async-done(((bf16[16,3,16,256]{3,2,1,0:T(8,128)(2,1)}), bf16[16,3,16,256]{3,2,1,0:T(8,128)(2,1)S(1)}, u32[]{:S(2)}, u32[]{:S(2)}) %all-to-all-start.4) | async-done | bytes 393248 | tf_op jit(solution)/shard_map/all_to_all | solution.py:78
  191.7 3.7 %fusion.66 = f32[48,16,256]{2,1,0:T(8,128)S(1)} fusion(bf16[48,256,256]{2,1,0:T(8,128)(2,1)} %param.29, bf16[48,16,256]{2,1,0:T(8,128)(2,1)S(1)} %gather_fusion.7, pred[48]{0:T(512)(128)(4,1)S(1)} %get-tuple-element.10), kind=kOutput, calls=%fused_computation.90 | convolution fusion | flops 100859904 | bytes 7471152 | tf_op jit(solution)/shard_map/ltp,lpq->ltq/dot_general | solution.py:92
  197.8 31.4 %psum.45 = f32[8,16]{1,0:T(8,128)S(1)} all-reduce(f32[8,16]{1,0:T(8,128)S(1)} %broadcast_select_fusion.8), channel_id=1, replica_groups=mesh['runs'=2,'area'=16] {'area'}, use_global_device_ids=true, to_apply=%region_17.21 | all-reduce | flops 128 | bytes 1024 | tf_op jit(solution)/shard_map/psum | solution.py:85
  230.2 3.7 %all-to-all-start.5 = ((bf16[16,3,16,256]{3,2,1,0:T(8,128)(2,1)}), bf16[16,3,16,256]{3,2,1,0:T(8,128)(2,1)S(1)}, u32[]{:S(2)}, u32[]{:S(2)}) async-start(bf16[16,3,16,256]{3,2,1,0:T(8,128)(2,1)} %bitcast.18), calls=%async_computation.5 | async-start | bytes 786432 | tf_op jit(solution)/shard_map/all_to_all | solution.py:78
  235.3 10.5 %all-to-all-done.5 = bf16[16,3,16,256]{3,2,1,0:T(8,128)(2,1)S(1)} async-done(((bf16[16,3,16,256]{3,2,1,0:T(8,128)(2,1)}), bf16[16,3,16,256]{3,2,1,0:T(8,128)(2,1)S(1)}, u32[]{:S(2)}, u32[]{:S(2)}) %all-to-all-start.5) | async-done | bytes 393248 | tf_op jit(solution)/shard_map/all_to_all | solution.py:78
  246.5 3.7 %fusion.64 = f32[48,16,256]{2,1,0:T(8,128)S(1)} fusion(bf16[48,256,256]{2,1,0:T(8,128)(2,1)} %param.29, bf16[48,16,256]{2,1,0:T(8,128)(2,1)S(1)} %gather_fusion.10, pred[48]{0:T(512)(128)(4,1)S(1)} %get-tuple-element.10), kind=kOutput, calls=%fused_computation.88 | convolution fusion | flops 100859904 | bytes 7471152 | tf_op jit(solution)/shard_map/ltp,lpq->ltq/dot_general | solution.py:92
  252.5 31.4 %psum.46 = f32[8,16]{1,0:T(8,128)S(1)} all-reduce(f32[8,16]{1,0:T(8,128)S(1)} %broadcast_select_fusion.7), channel_id=1, replica_groups=mesh['runs'=2,'area'=16] {'area'}, use_global_device_ids=true, to_apply=%region_20.24 | all-reduce | flops 128 | bytes 1024 | tf_op jit(solution)/shard_map/psum | solution.py:85
  289.9 10.7 %all-to-all-done.6 = bf16[16,3,16,256]{3,2,1,0:T(8,128)(2,1)S(1)} async-done(((bf16[16,3,16,256]{3,2,1,0:T(8,128)(2,1)}), bf16[16,3,16,256]{3,2,1,0:T(8,128)(2,1)S(1)}, u32[]{:S(2)}, u32[]{:S(2)}) %all-to-all-start.6) | async-done | bytes 393248 | tf_op jit(solution)/shard_map/all_to_all | solution.py:78
  301.2 3.7 %fusion.62 = f32[48,16,256]{2,1,0:T(8,128)S(1)} fusion(bf16[48,256,256]{2,1,0:T(8,128)(2,1)} %param.29, bf16[48,16,256]{2,1,0:T(8,128)(2,1)S(1)} %gather_fusion.13, pred[48]{0:T(512)(128)(4,1)S(1)} %get-tuple-element.10), kind=kOutput, calls=%fused_computation.86 | convolution fusion | flops 100859904 | bytes 7471152 | tf_op jit(solution)/shard_map/ltp,lpq->ltq/dot_general | solution.py:92
  307.2 31.4 %psum.47 = f32[8,16]{1,0:T(8,128)S(1)} all-reduce(f32[8,16]{1,0:T(8,128)S(1)} %broadcast_select_fusion.6), channel_id=1, replica_groups=mesh['runs'=2,'area'=16] {'area'}, use_global_device_ids=true, to_apply=%region_23.27 | all-reduce | flops 128 | bytes 1024 | tf_op jit(solution)/shard_map/psum | solution.py:85
  344.6 10.7 %all-to-all-done.7 = bf16[16,3,16,256]{3,2,1,0:T(8,128)(2,1)S(1)} async-done(((bf16[16,3,16,256]{3,2,1,0:T(8,128)(2,1)}), bf16[16,3,16,256]{3,2,1,0:T(8,128)(2,1)S(1)}, u32[]{:S(2)}, u32[]{:S(2)}) %all-to-all-start.7) | async-done | bytes 393248 | tf_op jit(solution)/shard_map/all_to_all | solution.py:78
  355.9 3.7 %fusion.60 = f32[48,16,256]{2,1,0:T(8,128)S(1)} fusion(bf16[48,256,256]{2,1,0:T(8,128)(2,1)} %param.29, bf16[48,16,256]{2,1,0:T(8,128)(2,1)S(1)} %gather_fusion.16, pred[48]{0:T(512)(128)(4,1)S(1)} %get-tuple-element.10), kind=kOutput, calls=%fused_computation.84 | convolution fusion | flops 100859904 | bytes 7471152 | tf_op jit(solution)/shard_map/ltp,lpq->ltq/dot_general | solution.py:92
  (115 shorter events, 56.8 us)
Async XLA Ops:
  0.0 70.1 %copy-start = (bf16[16,256,256]{2,1,0:T(8,128)(2,1)S(1)}, bf16[16,256,256]{2,1,0:T(8,128)(2,1)}, u32[]{:S(2)}) copy-start(bf16[16,256,256]{2,1,0:T(8,128)(2,1)} %param.33) | copy-start | bytes 6291460
  3.1 51.3 %all-to-all-start.1 = ((s32[16,1,3]{2,1,0:T(1,128)}), s32[16,1,3]{2,1,0:T(1,128)S(1)}, u32[]{:S(2)}, u32[]{:S(2)}) async-start(s32[16,1,3]{2,1,0:T(1,128)} %bitcast.6), calls=%async_computation.1 | async-start | bytes 16384 | tf_op jit(solution)/shard_map/all_to_all | solution.py:50
  54.4 9.9 %all-to-all-start = ((s32[16,1,3]{2,1,0:T(1,128)}), s32[16,1,3]{2,1,0:T(1,128)S(1)}, u32[]{:S(2)}, u32[]{:S(2)}) async-start(s32[16,1,3]{2,1,0:T(1,128)} %bitcast.5), calls=%async_computation | async-start | bytes 16384 | tf_op jit(solution)/shard_map/all_to_all | solution.py:53
  65.1 20.9 %copy-start.2 = (s32[48]{0:T(128)S(1)}, s32[48]{0:T(128)}, u32[]{:S(2)}) copy-start(s32[48]{0:T(128)} %param.27) | copy-start | bytes 580
  65.9 15.7 %all-to-all-start.2 = ((bf16[16,3,16,256]{3,2,1,0:T(8,128)(2,1)}), bf16[16,3,16,256]{3,2,1,0:T(8,128)(2,1)S(1)}, u32[]{:S(2)}, u32[]{:S(2)}) async-start(bf16[16,3,16,256]{3,2,1,0:T(8,128)(2,1)} %bitcast.8), calls=%async_computation.2 | async-start | bytes 786432 | tf_op jit(solution)/shard_map/all_to_all | solution.py:78
  82.2 43.1 %copy-start.1 = (s32[16]{0:T(128)S(1)}, s32[16]{0:T(128)}, u32[]{:S(2)}) copy-start(s32[16]{0:T(128)} %param.31) | copy-start | bytes 196
  120.7 15.7 %all-to-all-start.3 = ((bf16[16,3,16,256]{3,2,1,0:T(8,128)(2,1)}), bf16[16,3,16,256]{3,2,1,0:T(8,128)(2,1)S(1)}, u32[]{:S(2)}, u32[]{:S(2)}) async-start(bf16[16,3,16,256]{3,2,1,0:T(8,128)(2,1)} %bitcast.14), calls=%async_computation.3 | async-start | bytes 786432 | tf_op jit(solution)/shard_map/all_to_all | solution.py:78
  175.4 15.7 %all-to-all-start.4 = ((bf16[16,3,16,256]{3,2,1,0:T(8,128)(2,1)}), bf16[16,3,16,256]{3,2,1,0:T(8,128)(2,1)S(1)}, u32[]{:S(2)}, u32[]{:S(2)}) async-start(bf16[16,3,16,256]{3,2,1,0:T(8,128)(2,1)} %bitcast.16), calls=%async_computation.4 | async-start | bytes 786432 | tf_op jit(solution)/shard_map/all_to_all | solution.py:78
  230.2 15.7 %all-to-all-start.5 = ((bf16[16,3,16,256]{3,2,1,0:T(8,128)(2,1)}), bf16[16,3,16,256]{3,2,1,0:T(8,128)(2,1)S(1)}, u32[]{:S(2)}, u32[]{:S(2)}) async-start(bf16[16,3,16,256]{3,2,1,0:T(8,128)(2,1)} %bitcast.18), calls=%async_computation.5 | async-start | bytes 786432 | tf_op jit(solution)/shard_map/all_to_all | solution.py:78
  284.9 15.7 %all-to-all-start.6 = ((bf16[16,3,16,256]{3,2,1,0:T(8,128)(2,1)}), bf16[16,3,16,256]{3,2,1,0:T(8,128)(2,1)S(1)}, u32[]{:S(2)}, u32[]{:S(2)}) async-start(bf16[16,3,16,256]{3,2,1,0:T(8,128)(2,1)} %bitcast.20), calls=%async_computation.6 | async-start | bytes 786432 | tf_op jit(solution)/shard_map/all_to_all | solution.py:78
  339.6 15.7 %all-to-all-start.7 = ((bf16[16,3,16,256]{3,2,1,0:T(8,128)(2,1)}), bf16[16,3,16,256]{3,2,1,0:T(8,128)(2,1)S(1)}, u32[]{:S(2)}, u32[]{:S(2)}) async-start(bf16[16,3,16,256]{3,2,1,0:T(8,128)(2,1)} %bitcast.22), calls=%async_computation.7 | async-start | bytes 786432 | tf_op jit(solution)/shard_map/all_to_all | solution.py:78
where the time goes:
time: 363 us; the launch traced here: 361 us
  blocking collectives  191 us (53%)
  waiting for transfers between devices  67.9 us (19%)
  matrix products  33.8 us (9%)
  starting transfers between devices  32.4 us (9%)
  other arithmetic  18.7 us (5%)
  local copies, waits for them, and re-layouts  16.2 us (4%)
    psum x6, blocking collectives, local(): summed = lax.psum(area_table, 'area')  191 us
    all_to_all x6, waiting for transfers between devices, local(): lax.all_to_all(outgoing, 'area', split_axis=0, concat_axis=0, tiled=True)  63.5 us
    dot_general x6, matrix products, local(): jnp.einsum('ltp,lpq->ltq', remote_in, remote_weight, preferred_element_ty...  22.5 us
    all_to_all x6, starting transfers between devices, local(): lax.all_to_all(outgoing, 'area', split_axis=0, concat_axis=0, tiled=True)  21.5 us
    all_to_all x1, starting transfers between devices, local(): lax.all_to_all(want_block.reshape(devices, capacity), 'area', split_axis=...  7.39 us
  transfers between devices with their start and end apart: 8, of which 7 were waited for; matrix products, arithmetic and copies ran while one was open for 6% of the time, Pallas kernels for 0%

commit v1 on v0

--- a/solution.py
+++ b/solution.py
@@ -4,6 +4,14 @@
 from jax.sharding import PartitionSpec as P
 
 STEPS = 6
+
+
+def doubling_sum(value, axis):
+    size, total = (lax.axis_size(axis), value)
+    for far in [1 << k for k in range(size.bit_length() - 1)]:
+        swap = [(i, i ^ far) for i in range(size)]
+        total = total + lax.ppermute(total, axis, swap)
+    return total
 
 
 def local(
@@ -82,7 +90,7 @@
         previous = state_rows[:blocks].astype(jnp.float32)
         own_sum = jnp.sum(previous, axis=(0, 2))
         area_table = jnp.where(area_mask[:, None], own_sum[None, :], 0.0)
-        summed = lax.psum(area_table, "area")
+        summed = doubling_sum(area_table, "area")
         total_mine = jnp.sum(jnp.where(area_mask[:, None], summed, 0.0), axis=0)
         mean_now = total_mine / area_count
         local_in = jnp.take(state_rows, local_index, axis=0)

time: 363 us -> 198 us (0.55)
  blocking collectives: 191 us -> 0 us
  starting transfers between devices: 32.4 us -> 84.4 us
  waiting for transfers between devices: 67.9 us -> 43.6 us
    psum x6 -> x0, blocking collectives: 191 us -> none  [local(): summed = lax.psum(area_table, 'area')]
    all_to_all x6, waiting for transfers between devices: 63.5 us -> 0.02 us  [local(): lax.all_to_all(outgoing, 'area', split_axis=0, concat_axis=0, tiled=True)]
    ppermute x0 -> x24, starting transfers between devices: none -> 46.5 us  [doubling_sum(): total = total + lax.ppermute(total, axis, swap)]
    ppermute x0 -> x24, waiting for transfers between devices: none -> 39.1 us  [doubling_sum(): total = total + lax.ppermute(total, axis, swap)]
  transfers between devices with their start and end apart: 8 -> 32, of which waited for: 7 -> 13; matrix products, arithmetic and copies ran while one was open for 6% -> 16% of each run, Pallas kernels for 0% -> 0%
where the time goes in v1:
time: 198 us; the launch traced here: 197 us
  starting transfers between devices  84.4 us (43%)
  waiting for transfers between devices  43.6 us (22%)
  matrix products  33.7 us (17%)
  other arithmetic  18.8 us (9%)
  local copies, waits for them, and re-layouts  15.4 us (8%)
    ppermute x24, starting transfers between devices, doubling_sum(): total = total + lax.ppermute(total, axis, swap)  46.5 us
    ppermute x24, waiting for transfers between devices, doubling_sum(): total = total + lax.ppermute(total, axis, swap)  39.1 us
    all_to_all x6, starting transfers between devices, local(): lax.all_to_all(outgoing, 'area', split_axis=0, concat_axis=0, tiled=True)  24.7 us
    dot_general x6, matrix products, local(): jnp.einsum('ltp,lpq->ltq', remote_in, remote_weight, preferred_element_ty...  22.5 us
    all_to_all x1, starting transfers between devices, local(): lax.all_to_all(want_block.reshape(devices, capacity), 'area', split_axis=...  7.39 us
    dot_general x6, matrix products, local(): jnp.einsum('bl,ltq->btq', target_onehot, remote_terms, precision=lax.Prec...  5.92 us
    all_to_all x1, starting transfers between devices, local(): lax.all_to_all(want_delay.reshape(devices, capacity), 'area', split_axis=...  5.76 us
    select_n x7, other arithmetic, local(): jnp.take(state_rows, (asked_delay - 1) * blocks + asked_block, axis=0)  5.15 us
  transfers between devices with their start and end apart: 32, of which 13 were waited for; matrix products, arithmetic and copies ran while one was open for 16% of the time, Pallas kernels for 0%

profile of v1, /device:TPU:0, one launch (start us, length us, event | category | flops | bytes accessed | tf_op | source)
XLA Modules:
  0.0 197.2 jit_solution(11606033375594691733)
XLA Ops:
  3.1 7.4 %all-to-all-start.1 = ((s32[16,1,3]{2,1,0:T(1,128)}), s32[16,1,3]{2,1,0:T(1,128)S(1)}, u32[]{:S(2)}, u32[]{:S(2)}) async-start(s32[16,1,3]{2,1,0:T(1,128)} %bitcast.6), calls=%async_computation.1 | async-start | bytes 16384 | tf_op jit(solution)/shard_map/all_to_all | solution.py:58
  18.9 5.8 %all-to-all-start = ((s32[16,1,3]{2,1,0:T(1,128)}), s32[16,1,3]{2,1,0:T(1,128)S(1)}, u32[]{:S(2)}, u32[]{:S(2)}) async-start(s32[16,1,3]{2,1,0:T(1,128)} %bitcast.5), calls=%async_computation | async-start | bytes 16384 | tf_op jit(solution)/shard_map/all_to_all | solution.py:61
  26.6 4.5 %all-to-all-done = s32[16,1,3]{2,1,0:T(1,128)S(1)} async-done(((s32[16,1,3]{2,1,0:T(1,128)}), s32[16,1,3]{2,1,0:T(1,128)S(1)}, u32[]{:S(2)}, u32[]{:S(2)}) %all-to-all-start) | async-done | bytes 224 | tf_op jit(solution)/shard_map/all_to_all | solution.py:61
  38.7 5.5 %collective-permute-done.2 = f32[8,16]{1,0:T(8,128)S(1)} collective-permute-done((f32[8,16]{1,0:T(8,128)S(1)}, f32[8,16]{1,0:T(8,128)S(1)}, u32[]{:S(2)}, u32[]{:S(2)}) %collective-permute-start.2) | collective-permute-done | bytes 544 | tf_op jit(solution)/shard_map/ppermute | solution.py:13
  44.2 4.5 %collective-permute-start.3 = (f32[8,16]{1,0:T(8,128)S(1)}, f32[8,16]{1,0:T(8,128)S(1)}, u32[]{:S(2)}, u32[]{:S(2)}) collective-permute-start(f32[8,16]{1,0:T(8,128)S(1)} %add.195), channel_id=1, source_target_pairs={{0,8},{1,9},{2,10},{3,11},{4,12},{5,13},{6,14},{7,15},{8,0},{9,1},... | collective-permute-start | bytes 1544 | tf_op jit(solution)/shard_map/ppermute | solution.py:13
  52.0 3.8 %fusion.70 = f32[48,16,256]{2,1,0:T(8,128)S(1)} fusion(bf16[48,256,256]{2,1,0:T(8,128)(2,1)} %param.29, bf16[48,16,256]{2,1,0:T(8,128)(2,1)S(1)} %gather_fusion.1, pred[48]{0:T(512)(128)(4,1)S(1)} %get-tuple-element.10), kind=kOutput, calls=%fused_computation.94 | convolution fusion | flops 100859904 | bytes 7471152 | tf_op jit(solution)/shard_map/ltp,lpq->ltq/dot_general | solution.py:100
  60.9 3.9 %all-to-all-start.3 = ((bf16[16,3,16,256]{3,2,1,0:T(8,128)(2,1)}), bf16[16,3,16,256]{3,2,1,0:T(8,128)(2,1)S(1)}, u32[]{:S(2)}, u32[]{:S(2)}) async-start(bf16[16,3,16,256]{3,2,1,0:T(8,128)(2,1)} %bitcast.14), calls=%async_computation.3 | async-start | bytes 786432 | tf_op jit(solution)/shard_map/all_to_all | solution.py:86
  67.2 5.1 %collective-permute-done.6 = f32[8,16]{1,0:T(8,128)S(1)} collective-permute-done((f32[8,16]{1,0:T(8,128)S(1)}, f32[8,16]{1,0:T(8,128)S(1)}, u32[]{:S(2)}, u32[]{:S(2)}) %collective-permute-start.6) | collective-permute-done | bytes 544 | tf_op jit(solution)/shard_map/ppermute | solution.py:13
  72.3 4.4 %collective-permute-start.7 = (f32[8,16]{1,0:T(8,128)S(1)}, f32[8,16]{1,0:T(8,128)S(1)}, u32[]{:S(2)}, u32[]{:S(2)}) collective-permute-start(f32[8,16]{1,0:T(8,128)S(1)} %add.203), channel_id=1, source_target_pairs={{0,8},{1,9},{2,10},{3,11},{4,12},{5,13},{6,14},{7,15},{8,0},{9,1},... | collective-permute-start | bytes 1544 | tf_op jit(solution)/shard_map/ppermute | solution.py:13
  79.7 3.7 %fusion.68 = f32[48,16,256]{2,1,0:T(8,128)S(1)} fusion(bf16[48,256,256]{2,1,0:T(8,128)(2,1)} %param.29, bf16[48,16,256]{2,1,0:T(8,128)(2,1)S(1)} %gather_fusion.4, pred[48]{0:T(512)(128)(4,1)S(1)} %get-tuple-element.10), kind=kOutput, calls=%fused_computation.92 | convolution fusion | flops 100859904 | bytes 7471152 | tf_op jit(solution)/shard_map/ltp,lpq->ltq/dot_general | solution.py:100
  88.6 4.3 %all-to-all-start.4 = ((bf16[16,3,16,256]{3,2,1,0:T(8,128)(2,1)}), bf16[16,3,16,256]{3,2,1,0:T(8,128)(2,1)S(1)}, u32[]{:S(2)}, u32[]{:S(2)}) async-start(bf16[16,3,16,256]{3,2,1,0:T(8,128)(2,1)} %bitcast.16), calls=%async_computation.4 | async-start | bytes 786432 | tf_op jit(solution)/shard_map/all_to_all | solution.py:86
  95.3 5.1 %collective-permute-done.10 = f32[8,16]{1,0:T(8,128)S(1)} collective-permute-done((f32[8,16]{1,0:T(8,128)S(1)}, f32[8,16]{1,0:T(8,128)S(1)}, u32[]{:S(2)}, u32[]{:S(2)}) %collective-permute-start.10) | collective-permute-done | bytes 544 | tf_op jit(solution)/shard_map/ppermute | solution.py:13
  100.4 4.4 %collective-permute-start.11 = (f32[8,16]{1,0:T(8,128)S(1)}, f32[8,16]{1,0:T(8,128)S(1)}, u32[]{:S(2)}, u32[]{:S(2)}) collective-permute-start(f32[8,16]{1,0:T(8,128)S(1)} %add.211), channel_id=1, source_target_pairs={{0,8},{1,9},{2,10},{3,11},{4,12},{5,13},{6,14},{7,15},{8,0},{9,1},... | collective-permute-start | bytes 1544 | tf_op jit(solution)/shard_map/ppermute | solution.py:13
  107.7 3.7 %fusion.66 = f32[48,16,256]{2,1,0:T(8,128)S(1)} fusion(bf16[48,256,256]{2,1,0:T(8,128)(2,1)} %param.29, bf16[48,16,256]{2,1,0:T(8,128)(2,1)S(1)} %gather_fusion.7, pred[48]{0:T(512)(128)(4,1)S(1)} %get-tuple-element.10), kind=kOutput, calls=%fused_computation.90 | convolution fusion | flops 100859904 | bytes 7471152 | tf_op jit(solution)/shard_map/ltp,lpq->ltq/dot_general | solution.py:100
  116.6 4.3 %all-to-all-start.5 = ((bf16[16,3,16,256]{3,2,1,0:T(8,128)(2,1)}), bf16[16,3,16,256]{3,2,1,0:T(8,128)(2,1)S(1)}, u32[]{:S(2)}, u32[]{:S(2)}) async-start(bf16[16,3,16,256]{3,2,1,0:T(8,128)(2,1)} %bitcast.18), calls=%async_computation.5 | async-start | bytes 786432 | tf_op jit(solution)/shard_map/all_to_all | solution.py:86
  123.3 5.1 %collective-permute-done.14 = f32[8,16]{1,0:T(8,128)S(1)} collective-permute-done((f32[8,16]{1,0:T(8,128)S(1)}, f32[8,16]{1,0:T(8,128)S(1)}, u32[]{:S(2)}, u32[]{:S(2)}) %collective-permute-start.14) | collective-permute-done | bytes 544 | tf_op jit(solution)/shard_map/ppermute | solution.py:13
  128.4 4.4 %collective-permute-start.15 = (f32[8,16]{1,0:T(8,128)S(1)}, f32[8,16]{1,0:T(8,128)S(1)}, u32[]{:S(2)}, u32[]{:S(2)}) collective-permute-start(f32[8,16]{1,0:T(8,128)S(1)} %add.219), channel_id=1, source_target_pairs={{0,8},{1,9},{2,10},{3,11},{4,12},{5,13},{6,14},{7,15},{8,0},{9,1},... | collective-permute-start | bytes 1544 | tf_op jit(solution)/shard_map/ppermute | solution.py:13
  144.7 4.3 %all-to-all-start.6 = ((bf16[16,3,16,256]{3,2,1,0:T(8,128)(2,1)}), bf16[16,3,16,256]{3,2,1,0:T(8,128)(2,1)S(1)}, u32[]{:S(2)}, u32[]{:S(2)}) async-start(bf16[16,3,16,256]{3,2,1,0:T(8,128)(2,1)} %bitcast.20), calls=%async_computation.6 | async-start | bytes 786432 | tf_op jit(solution)/shard_map/all_to_all | solution.py:86
  151.4 5.1 %collective-permute-done.18 = f32[8,16]{1,0:T(8,128)S(1)} collective-permute-done((f32[8,16]{1,0:T(8,128)S(1)}, f32[8,16]{1,0:T(8,128)S(1)}, u32[]{:S(2)}, u32[]{:S(2)}) %collective-permute-start.18) | collective-permute-done | bytes 544 | tf_op jit(solution)/shard_map/ppermute | solution.py:13
  156.5 4.4 %collective-permute-start.19 = (f32[8,16]{1,0:T(8,128)S(1)}, f32[8,16]{1,0:T(8,128)S(1)}, u32[]{:S(2)}, u32[]{:S(2)}) collective-permute-start(f32[8,16]{1,0:T(8,128)S(1)} %add.227), channel_id=1, source_target_pairs={{0,8},{1,9},{2,10},{3,11},{4,12},{5,13},{6,14},{7,15},{8,0},{9,1},... | collective-permute-start | bytes 1544 | tf_op jit(solution)/shard_map/ppermute | solution.py:13
  163.8 3.7 %fusion.62 = f32[48,16,256]{2,1,0:T(8,128)S(1)} fusion(bf16[48,256,256]{2,1,0:T(8,128)(2,1)} %param.29, bf16[48,16,256]{2,1,0:T(8,128)(2,1)S(1)} %gather_fusion.13, pred[48]{0:T(512)(128)(4,1)S(1)} %get-tuple-element.10), kind=kOutput, calls=%fused_computation.86 | convolution fusion | flops 100859904 | bytes 7471152 | tf_op jit(solution)/shard_map/ltp,lpq->ltq/dot_general | solution.py:100
  172.8 4.3 %all-to-all-start.7 = ((bf16[16,3,16,256]{3,2,1,0:T(8,128)(2,1)}), bf16[16,3,16,256]{3,2,1,0:T(8,128)(2,1)S(1)}, u32[]{:S(2)}, u32[]{:S(2)}) async-start(bf16[16,3,16,256]{3,2,1,0:T(8,128)(2,1)} %bitcast.22), calls=%async_computation.7 | async-start | bytes 786432 | tf_op jit(solution)/shard_map/all_to_all | solution.py:86
  179.6 5.1 %collective-permute-done.22 = f32[8,16]{1,0:T(8,128)S(1)} collective-permute-done((f32[8,16]{1,0:T(8,128)S(1)}, f32[8,16]{1,0:T(8,128)S(1)}, u32[]{:S(2)}, u32[]{:S(2)}) %collective-permute-start.22) | collective-permute-done | bytes 544 | tf_op jit(solution)/shard_map/ppermute | solution.py:13
  184.6 4.4 %collective-permute-start.23 = (f32[8,16]{1,0:T(8,128)S(1)}, f32[8,16]{1,0:T(8,128)S(1)}, u32[]{:S(2)}, u32[]{:S(2)}) collective-permute-start(f32[8,16]{1,0:T(8,128)S(1)} %add.235), channel_id=1, source_target_pairs={{0,8},{1,9},{2,10},{3,11},{4,12},{5,13},{6,14},{7,15},{8,0},{9,1},... | collective-permute-start | bytes 1544 | tf_op jit(solution)/shard_map/ppermute | solution.py:13
  (179 shorter events, 84.3 us)
Async XLA Ops:
  3.1 15.7 %all-to-all-start.1 = ((s32[16,1,3]{2,1,0:T(1,128)}), s32[16,1,3]{2,1,0:T(1,128)S(1)}, u32[]{:S(2)}, u32[]{:S(2)}) async-start(s32[16,1,3]{2,1,0:T(1,128)} %bitcast.6), calls=%async_computation.1 | async-start | bytes 16384 | tf_op jit(solution)/shard_map/all_to_all | solution.py:58
  13.6 18.3 %collective-permute-start = (f32[8,16]{1,0:T(8,128)S(1)}, f32[8,16]{1,0:T(8,128)S(1)}, u32[]{:S(2)}, u32[]{:S(2)}) collective-permute-start(f32[8,16]{1,0:T(8,128)S(1)} %broadcast_select_fusion.11), channel_id=1, source_target_pairs={{0,1},{1,0},{2,3},{3,2},{4,5},{5,4},{6,7},{7,6},{8,9},{9,8},{10,11... | collective-permute-start | bytes 1544 | tf_op jit(solution)/shard_map/ppermute | solution.py:13
  18.9 12.2 %all-to-all-start = ((s32[16,1,3]{2,1,0:T(1,128)}), s32[16,1,3]{2,1,0:T(1,128)S(1)}, u32[]{:S(2)}, u32[]{:S(2)}) async-start(s32[16,1,3]{2,1,0:T(1,128)} %bitcast.5), calls=%async_computation | async-start | bytes 16384 | tf_op jit(solution)/shard_map/all_to_all | solution.py:61
  33.3 18.1 %all-to-all-start.2 = ((bf16[16,3,16,256]{3,2,1,0:T(8,128)(2,1)}), bf16[16,3,16,256]{3,2,1,0:T(8,128)(2,1)S(1)}, u32[]{:S(2)}, u32[]{:S(2)}) async-start(bf16[16,3,16,256]{3,2,1,0:T(8,128)(2,1)} %bitcast.8), calls=%async_computation.2 | async-start | bytes 786432 | tf_op jit(solution)/shard_map/all_to_all | solution.py:86
  36.9 7.3 %collective-permute-start.2 = (f32[8,16]{1,0:T(8,128)S(1)}, f32[8,16]{1,0:T(8,128)S(1)}, u32[]{:S(2)}, u32[]{:S(2)}) collective-permute-start(f32[8,16]{1,0:T(8,128)S(1)} %fusion.179), channel_id=1, source_target_pairs={{0,4},{1,5},{2,6},{3,7},{4,0},{5,1},{6,2},{7,3},{8,12},{9,13},{10,... | collective-permute-start | bytes 1544 | tf_op jit(solution)/shard_map/ppermute | solution.py:13
  44.2 6.4 %collective-permute-start.3 = (f32[8,16]{1,0:T(8,128)S(1)}, f32[8,16]{1,0:T(8,128)S(1)}, u32[]{:S(2)}, u32[]{:S(2)}) collective-permute-start(f32[8,16]{1,0:T(8,128)S(1)} %add.195), channel_id=1, source_target_pairs={{0,8},{1,9},{2,10},{3,11},{4,12},{5,13},{6,14},{7,15},{8,0},{9,1},... | collective-permute-start | bytes 1544 | tf_op jit(solution)/shard_map/ppermute | solution.py:13
  58.5 6.3 %collective-permute-start.5 = (f32[8,16]{1,0:T(8,128)S(1)}, f32[8,16]{1,0:T(8,128)S(1)}, u32[]{:S(2)}, u32[]{:S(2)}) collective-permute-start(f32[8,16]{1,0:T(8,128)S(1)} %fusion.130), channel_id=1, source_target_pairs={{0,2},{1,3},{2,0},{3,1},{4,6},{5,7},{6,4},{7,5},{8,10},{9,11},{10,... | collective-permute-start | bytes 1544 | tf_op jit(solution)/shard_map/ppermute | solution.py:13
  60.9 18.2 %all-to-all-start.3 = ((bf16[16,3,16,256]{3,2,1,0:T(8,128)(2,1)}), bf16[16,3,16,256]{3,2,1,0:T(8,128)(2,1)S(1)}, u32[]{:S(2)}, u32[]{:S(2)}) async-start(bf16[16,3,16,256]{3,2,1,0:T(8,128)(2,1)} %bitcast.14), calls=%async_computation.3 | async-start | bytes 786432 | tf_op jit(solution)/shard_map/all_to_all | solution.py:86
  64.9 7.4 %collective-permute-start.6 = (f32[8,16]{1,0:T(8,128)S(1)}, f32[8,16]{1,0:T(8,128)S(1)}, u32[]{:S(2)}, u32[]{:S(2)}) collective-permute-start(f32[8,16]{1,0:T(8,128)S(1)} %fusion.178), channel_id=1, source_target_pairs={{0,4},{1,5},{2,6},{3,7},{4,0},{5,1},{6,2},{7,3},{8,12},{9,13},{10,... | collective-permute-start | bytes 1544 | tf_op jit(solution)/shard_map/ppermute | solution.py:13
  86.3 6.6 %collective-permute-start.9 = (f32[8,16]{1,0:T(8,128)S(1)}, f32[8,16]{1,0:T(8,128)S(1)}, u32[]{:S(2)}, u32[]{:S(2)}) collective-permute-start(f32[8,16]{1,0:T(8,128)S(1)} %fusion.131), channel_id=1, source_target_pairs={{0,2},{1,3},{2,0},{3,1},{4,6},{5,7},{6,4},{7,5},{8,10},{9,11},{10,... | collective-permute-start | bytes 1544 | tf_op jit(solution)/shard_map/ppermute | solution.py:13
  88.6 18.6 %all-to-all-start.4 = ((bf16[16,3,16,256]{3,2,1,0:T(8,128)(2,1)}), bf16[16,3,16,256]{3,2,1,0:T(8,128)(2,1)S(1)}, u32[]{:S(2)}, u32[]{:S(2)}) async-start(bf16[16,3,16,256]{3,2,1,0:T(8,128)(2,1)} %bitcast.16), calls=%async_computation.4 | async-start | bytes 786432 | tf_op jit(solution)/shard_map/all_to_all | solution.py:86
  93.0 7.4 %collective-permute-start.10 = (f32[8,16]{1,0:T(8,128)S(1)}, f32[8,16]{1,0:T(8,128)S(1)}, u32[]{:S(2)}, u32[]{:S(2)}) collective-permute-start(f32[8,16]{1,0:T(8,128)S(1)} %fusion.177), channel_id=1, source_target_pairs={{0,4},{1,5},{2,6},{3,7},{4,0},{5,1},{6,2},{7,3},{8,12},{9,13},{10,... | collective-permute-start | bytes 1544 | tf_op jit(solution)/shard_map/ppermute | solution.py:13
  100.4 6.0 %collective-permute-start.11 = (f32[8,16]{1,0:T(8,128)S(1)}, f32[8,16]{1,0:T(8,128)S(1)}, u32[]{:S(2)}, u32[]{:S(2)}) collective-permute-start(f32[8,16]{1,0:T(8,128)S(1)} %add.211), channel_id=1, source_target_pairs={{0,8},{1,9},{2,10},{3,11},{4,12},{5,13},{6,14},{7,15},{8,0},{9,1},... | collective-permute-start | bytes 1544 | tf_op jit(solution)/shard_map/ppermute | solution.py:13
  114.3 6.6 %collective-permute-start.13 = (f32[8,16]{1,0:T(8,128)S(1)}, f32[8,16]{1,0:T(8,128)S(1)}, u32[]{:S(2)}, u32[]{:S(2)}) collective-permute-start(f32[8,16]{1,0:T(8,128)S(1)} %fusion.132), channel_id=1, source_target_pairs={{0,2},{1,3},{2,0},{3,1},{4,6},{5,7},{6,4},{7,5},{8,10},{9,11},{10,... | collective-permute-start | bytes 1544 | tf_op jit(solution)/shard_map/ppermute | solution.py:13
  116.6 18.6 %all-to-all-start.5 = ((bf16[16,3,16,256]{3,2,1,0:T(8,128)(2,1)}), bf16[16,3,16,256]{3,2,1,0:T(8,128)(2,1)S(1)}, u32[]{:S(2)}, u32[]{:S(2)}) async-start(bf16[16,3,16,256]{3,2,1,0:T(8,128)(2,1)} %bitcast.18), calls=%async_computation.5 | async-start | bytes 786432 | tf_op jit(solution)/shard_map/all_to_all | solution.py:86
  121.0 7.4 %collective-permute-start.14 = (f32[8,16]{1,0:T(8,128)S(1)}, f32[8,16]{1,0:T(8,128)S(1)}, u32[]{:S(2)}, u32[]{:S(2)}) collective-permute-start(f32[8,16]{1,0:T(8,128)S(1)} %fusion.176), channel_id=1, source_target_pairs={{0,4},{1,5},{2,6},{3,7},{4,0},{5,1},{6,2},{7,3},{8,12},{9,13},{10,... | collective-permute-start | bytes 1544 | tf_op jit(solution)/shard_map/ppermute | solution.py:13
  128.4 6.0 %collective-permute-start.15 = (f32[8,16]{1,0:T(8,128)S(1)}, f32[8,16]{1,0:T(8,128)S(1)}, u32[]{:S(2)}, u32[]{:S(2)}) collective-permute-start(f32[8,16]{1,0:T(8,128)S(1)} %add.219), channel_id=1, source_target_pairs={{0,8},{1,9},{2,10},{3,11},{4,12},{5,13},{6,14},{7,15},{8,0},{9,1},... | collective-permute-start | bytes 1544 | tf_op jit(solution)/shard_map/ppermute | solution.py:13
  142.3 6.6 %collective-permute-start.17 = (f32[8,16]{1,0:T(8,128)S(1)}, f32[8,16]{1,0:T(8,128)S(1)}, u32[]{:S(2)}, u32[]{:S(2)}) collective-permute-start(f32[8,16]{1,0:T(8,128)S(1)} %fusion.133), channel_id=1, source_target_pairs={{0,2},{1,3},{2,0},{3,1},{4,6},{5,7},{6,4},{7,5},{8,10},{9,11},{10,... | collective-permute-start | bytes 1544 | tf_op jit(solution)/shard_map/ppermute | solution.py:13
  144.7 18.6 %all-to-all-start.6 = ((bf16[16,3,16,256]{3,2,1,0:T(8,128)(2,1)}), bf16[16,3,16,256]{3,2,1,0:T(8,128)(2,1)S(1)}, u32[]{:S(2)}, u32[]{:S(2)}) async-start(bf16[16,3,16,256]{3,2,1,0:T(8,128)(2,1)} %bitcast.20), calls=%async_computation.6 | async-start | bytes 786432 | tf_op jit(solution)/shard_map/all_to_all | solution.py:86
  149.1 7.4 %collective-permute-start.18 = (f32[8,16]{1,0:T(8,128)S(1)}, f32[8,16]{1,0:T(8,128)S(1)}, u32[]{:S(2)}, u32[]{:S(2)}) collective-permute-start(f32[8,16]{1,0:T(8,128)S(1)} %fusion.175), channel_id=1, source_target_pairs={{0,4},{1,5},{2,6},{3,7},{4,0},{5,1},{6,2},{7,3},{8,12},{9,13},{10,... | collective-permute-start | bytes 1544 | tf_op jit(solution)/shard_map/ppermute | solution.py:13
  156.5 6.0 %collective-permute-start.19 = (f32[8,16]{1,0:T(8,128)S(1)}, f32[8,16]{1,0:T(8,128)S(1)}, u32[]{:S(2)}, u32[]{:S(2)}) collective-permute-start(f32[8,16]{1,0:T(8,128)S(1)} %add.227), channel_id=1, source_target_pairs={{0,8},{1,9},{2,10},{3,11},{4,12},{5,13},{6,14},{7,15},{8,0},{9,1},... | collective-permute-start | bytes 1544 | tf_op jit(solution)/shard_map/ppermute | solution.py:13
  169.9 7.2 %collective-permute-start.21 = (f32[8,16]{1,0:T(8,128)S(1)}, f32[8,16]{1,0:T(8,128)S(1)}, u32[]{:S(2)}, u32[]{:S(2)}) collective-permute-start(f32[8,16]{1,0:T(8,128)S(1)} %fusion.134), channel_id=1, source_target_pairs={{0,2},{1,3},{2,0},{3,1},{4,6},{5,7},{6,4},{7,5},{8,10},{9,11},{10,... | collective-permute-start | bytes 1544 | tf_op jit(solution)/shard_map/ppermute | solution.py:13
  172.8 18.6 %all-to-all-start.7 = ((bf16[16,3,16,256]{3,2,1,0:T(8,128)(2,1)}), bf16[16,3,16,256]{3,2,1,0:T(8,128)(2,1)S(1)}, u32[]{:S(2)}, u32[]{:S(2)}) async-start(bf16[16,3,16,256]{3,2,1,0:T(8,128)(2,1)} %bitcast.22), calls=%async_computation.7 | async-start | bytes 786432 | tf_op jit(solution)/shard_map/all_to_all | solution.py:86
  177.2 7.4 %collective-permute-start.22 = (f32[8,16]{1,0:T(8,128)S(1)}, f32[8,16]{1,0:T(8,128)S(1)}, u32[]{:S(2)}, u32[]{:S(2)}) collective-permute-start(f32[8,16]{1,0:T(8,128)S(1)} %fusion.174), channel_id=1, source_target_pairs={{0,4},{1,5},{2,6},{3,7},{4,0},{5,1},{6,2},{7,3},{8,12},{9,13},{10,... | collective-permute-start | bytes 1544 | tf_op jit(solution)/shard_map/ppermute | solution.py:13
  (13 other events, 193.6 us)
